TPU v7x, 128 devices: a whole 4x4x4 slice. The times are simulated.
128 devices in a mesh: row: 16 (over x, y), col: 8 (over z, core).
Axes of the slice: x: 4, y: 4, z: 4, core: 2. Of those that a mesh axis runs over, the one named last changes fastest.
Arguments:
- source_points: bfloat16 [65536, 1024], P('row'), may hold values from -8 to 8
- target_points: bfloat16 [32768, 1024], P('col', 'row'), may hold values from -8 to 8
- source_mass: float32 [65536], P('row'), may hold values from 0.25 to 4
- target_mass: float32 [32768], P('col'), may hold values from 0.25 to 4
- tile_index: int32 [256, 16], P('row', 'col'), may hold values from 0 to 15, as said below
- tile_count: int32 [256, 8], P('row', 'col'), may hold values from 1 to 2, as said below
Outputs:
- source_potential: float32 [65536], P('row')
- target_potential: float32 [32768], P('col')
Inputs may be any that keep to these rules, and one draw needn't show every extreme that they name: `tile_index`: within the 2 slots of one source tile and one index of col the target tiles are distinct; every target tile is named by a live slot of some source tile. `tile_count`: each index of row holds, for every index of col, a source tile with all 2 slots live.
All inputs are finite; a program needn't handle non-finite values.
Results may differ from a plain program's by a relative error of at most 0.0003.
Values may be sent and summed in bfloat16 or wider, within the bound.
A program may use at most 128 MiB of HBM per device.

v0:
```python
import math
import jax
import jax.numpy as jnp
from jax import lax
from jax.sharding import PartitionSpec as P

TILE = 256
ITERS = 3
masked_score = -1e30


def cost_terms(piece, source_points, tile_index):
    width = piece.shape[1]
    source_tiles = source_points.reshape(-1, TILE, width)
    target_tiles = piece.reshape(-1, TILE, width)
    chosen = target_tiles[tile_index]
    return jnp.einsum("rad,rkbd->rkab", source_tiles, chosen, preferred_element_type=jnp.float32)


def on_device(source_points, target_points, source_mass, target_mass, tile_index, tile_count):
    tiles_per_row = source_points.shape[0] // TILE
    col_tiles = target_points.shape[0] // TILE
    slot_count = tile_index.shape[1]
    scale = 1.0 / math.sqrt(source_points.shape[1])
    live = jnp.arange(slot_count)[None, :] < tile_count
    onehot = (tile_index[:, :, None] == jnp.arange(col_tiles)[None, None, :]) & live[:, :, None]
    log_source = jnp.log(source_mass).reshape(tiles_per_row, TILE)
    log_target = jnp.log(target_mass).reshape(col_tiles, TILE)
    target_pot = jnp.zeros((col_tiles, TILE), jnp.float32)
    source_pot = jnp.zeros((tiles_per_row, TILE), jnp.float32)
    for iteration in range(ITERS):
        cost = (
            cost_terms(
                lax.all_gather(target_points, "row", axis=1, tiled=True), source_points, tile_index
            )
            * scale
        )
        scores = cost + target_pot[tile_index][:, :, None, :]
        scores = jnp.where(live[:, :, None, None], scores, masked_score)
        row_top = jnp.max(scores, axis=(1, 3))
        highest = lax.pmax(row_top, "col")
        local_sum = jnp.sum(jnp.exp(scores - highest[:, None, :, None]), axis=(1, 3))
        total = lax.psum(local_sum, "col")
        source_pot = log_source - highest - jnp.log(total)
        columns = cost + source_pot[:, None, :, None]
        columns = jnp.where(live[:, :, None, None], columns, masked_score)
        slot_top = jnp.max(columns, axis=2)
        local_top = jnp.max(
            jnp.where(onehot[..., None], slot_top[:, :, None, :], masked_score), axis=(0, 1)
        )
        col_high = lax.pmax(local_top, "row")
        slot_ref = col_high[tile_index]
        sums = jnp.sum(jnp.exp(columns - slot_ref[:, :, None, :]), axis=2)
        col_sum = jnp.sum(jnp.where(onehot[..., None], sums[:, :, None, :], 0.0), axis=(0, 1))
        col_total = lax.psum(col_sum, "row")
        target_pot = log_target - col_high - jnp.log(col_total)
    return (source_pot.reshape(-1), target_pot.reshape(-1))


def solution(mesh):
    placed = (P("row", None), P("col", "row"), P("row"), P("col"), P("row", "col"), P("row", "col"))
    return jax.shard_map(
        on_device, mesh=mesh, in_specs=placed, out_specs=(P("row"), P("col")), check_vma=False
    )
```

profile of v0, /device:TPU:0, one launch (start us, length us, event | category | flops | bytes accessed | tf_op | source)
XLA Modules:
  0.0 747.5 jit_solution(9227641684370280702)
XLA Ops:
  7.2 0.7 all-gather.2.cloned.1.call-update
  7.9 0.8 copy.16
  8.7 0.7 compare_select_fusion
  9.5 0.6 gather_fusion.1
  10.2 0.7 log.24
  10.9 0.7 log.25
  11.6 0.7 iota_compare_fusion
  12.4 0.1 compare_and_fusion
  12.5 70.8 %all-gather.2.cloned.1.call-done = bf16[4096,1024]{0,1:T(8,128)(2,1)} async-done(((bf16[4096,64]{0,1:T(8,128)(2,1)}), bf16[4096,1024]{0,1:T(8,128)(2,1)}) %all-gather.2.cloned.1.call-update) | async-done | bytes 8388624 | tf_op jit(solution)/shard_map/all_gather | solution.py:34
  83.2 12.0 %copy.14 = bf16[4096,1024]{1,0:T(8,128)(2,1)} copy(bf16[4096,1024]{0,1:T(8,128)(2,1)} %all-gather.2.cloned.1.call-done) | data formatting | bytes 16777216 | tf_op jit(solution)/shard_map/all_gather | solution.py:34
  95.2 10.6 %gather_fusion = bf16[32,256,1024]{2,1,0:T(8,128)(2,1)} fusion(bf16[16,256,1024]{2,1,0:T(8,128)(2,1)} %bitcast.57, s32[1024]{0:T(1024)S(1)} %pad_clamp_fusion), kind=kCustom, calls=%fused_computation | custom fusion | bytes 33554560 | tf_op jit(solution)/shard_map/gather | solution.py:16
  105.8 13.5 %bitcast_reduce_fusion.5 = (f32[16,256]{1,0:T(8,128)S(1)}, f32[16,2,256,256]{3,2,1,0:T(8,128)}) fusion(f32[16,2,256]{2,1,0:T(2,128)S(1)} %reshape.108, pred[16,2]{1,0:T(8,128)(4,1)S(1)} %iota_compare_fusion, bf16[16,2,256,1024]{3,2,1,0:T(8,128)(2,1)} %bitcast.58, bf16[16,256,1024,1]{2,1,3,0:T(8,128)(2,1)} %bitcast.63), kind=kOutput, calls=%fused_computation.28 | convolution fusion | flops 4303351808 | bytes 33603616 | tf_op jit(solution)/shard_map/rad,rkbd->rkab/dot_general | solution.py:17
  119.3 25.8 %pmax.42 = f32[16,256]{1,0:T(8,128)S(1)} all-reduce(f32[16,256]{1,0:T(8,128)S(1)} %get-tuple-element.2), channel_id=1, replica_groups=mesh['row'=16,'col'=8] {'col'}, use_global_device_ids=true, to_apply=%region_1.2 | all-reduce | flops 4096 | bytes 32768 | tf_op jit(solution)/shard_map/pmax | solution.py:41
  145.1 4.6 fusion.11
  149.8 23.6 %psum.42 = f32[16,256]{1,0:T(8,128)S(1)} all-reduce(f32[16,256]{1,0:T(8,128)S(1)} %fusion.11), channel_id=1, replica_groups=mesh['row'=16,'col'=8] {'col'}, use_global_device_ids=true, to_apply=%region_3.4 | all-reduce | flops 4096 | bytes 32768 | tf_op jit(solution)/shard_map/psum | solution.py:43
  173.3 4.7 bitcast_reduce_fusion.4
  178.0 0.1 select_reduce_fusion.5
  178.1 72.4 %pmax.43 = f32[16,256]{1,0:T(8,128)S(1)} all-reduce(f32[16,256]{1,0:T(8,128)S(1)} %select_reduce_fusion.5), channel_id=1, replica_groups=mesh['row'=16,'col'=8] {'row'}, use_global_device_ids=true, to_apply=%region_6.7 | all-reduce | flops 4096 | bytes 32768 | tf_op jit(solution)/shard_map/pmax | solution.py:51
  250.5 0.6 gather_fusion.2
  251.1 5.1 fusion.9
  256.3 0.1 select_reduce_fusion.4
  256.4 69.5 %psum.43 = f32[16,256]{1,0:T(8,128)S(1)} all-reduce(f32[16,256]{1,0:T(8,128)S(1)} %select_reduce_fusion.4), channel_id=1, replica_groups=mesh['row'=16,'col'=8] {'row'}, use_global_device_ids=true, to_apply=%region_9.10 | all-reduce | flops 4096 | bytes 32768 | tf_op jit(solution)/shard_map/psum | solution.py:55
  326.0 0.6 gather_fusion.3
  326.6 4.4 bitcast_reduce_fusion.3
  331.0 23.7 %pmax.44 = f32[16,256]{1,0:T(8,128)S(1)} all-reduce(f32[16,256]{1,0:T(8,128)S(1)} %bitcast_reduce_fusion.3), channel_id=1, replica_groups=mesh['row'=16,'col'=8] {'col'}, use_global_device_ids=true, to_apply=%region_11.12 | all-reduce | flops 4096 | bytes 32768 | tf_op jit(solution)/shard_map/pmax | solution.py:41
  354.8 4.6 fusion.7
  359.4 23.6 %psum.44 = f32[16,256]{1,0:T(8,128)S(1)} all-reduce(f32[16,256]{1,0:T(8,128)S(1)} %fusion.7), channel_id=1, replica_groups=mesh['row'=16,'col'=8] {'col'}, use_global_device_ids=true, to_apply=%region_13.14 | all-reduce | flops 4096 | bytes 32768 | tf_op jit(solution)/shard_map/psum | solution.py:43
  383.0 4.7 bitcast_reduce_fusion.2
  387.6 0.1 select_reduce_fusion.3
  387.8 69.5 %pmax.45 = f32[16,256]{1,0:T(8,128)S(1)} all-reduce(f32[16,256]{1,0:T(8,128)S(1)} %select_reduce_fusion.3), channel_id=1, replica_groups=mesh['row'=16,'col'=8] {'row'}, use_global_device_ids=true, to_apply=%region_16.17 | all-reduce | flops 4096 | bytes 32768 | tf_op jit(solution)/shard_map/pmax | solution.py:51
  457.3 0.6 gather_fusion.4
  458.0 5.1 fusion.5
  463.1 0.1 select_reduce_fusion.2
  463.2 69.5 %psum.45 = f32[16,256]{1,0:T(8,128)S(1)} all-reduce(f32[16,256]{1,0:T(8,128)S(1)} %select_reduce_fusion.2), channel_id=1, replica_groups=mesh['row'=16,'col'=8] {'row'}, use_global_device_ids=true, to_apply=%region_19.20 | all-reduce | flops 4096 | bytes 32768 | tf_op jit(solution)/shard_map/psum | solution.py:55
  532.8 0.6 gather_fusion.5
  533.4 4.4 bitcast_reduce_fusion.1
  537.8 23.6 %pmax.46 = f32[16,256]{1,0:T(8,128)S(1)} all-reduce(f32[16,256]{1,0:T(8,128)S(1)} %bitcast_reduce_fusion.1), channel_id=1, replica_groups=mesh['row'=16,'col'=8] {'col'}, use_global_device_ids=true, to_apply=%region_21.22 | all-reduce | flops 4096 | bytes 32768 | tf_op jit(solution)/shard_map/pmax | solution.py:41
  561.4 4.6 fusion.3
  566.0 23.6 %psum.46 = f32[16,256]{1,0:T(8,128)S(1)} all-reduce(f32[16,256]{1,0:T(8,128)S(1)} %fusion.3), channel_id=1, replica_groups=mesh['row'=16,'col'=8] {'col'}, use_global_device_ids=true, to_apply=%region_23.24 | all-reduce | flops 4096 | bytes 32768 | tf_op jit(solution)/shard_map/psum | solution.py:43
  589.6 4.7 bitcast_reduce_fusion
  594.3 0.1 select_reduce_fusion.1
  594.4 69.5 %pmax.47 = f32[16,256]{1,0:T(8,128)S(1)} all-reduce(f32[16,256]{1,0:T(8,128)S(1)} %select_reduce_fusion.1), channel_id=1, replica_groups=mesh['row'=16,'col'=8] {'row'}, use_global_device_ids=true, to_apply=%region_26.27 | all-reduce | flops 4096 | bytes 32768 | tf_op jit(solution)/shard_map/pmax | solution.py:51
  663.9 0.6 gather_fusion.6
  664.6 5.1 fusion.1
  669.7 0.1 select_reduce_fusion
  669.8 69.5 %psum.47 = f32[16,256]{1,0:T(8,128)S(1)} all-reduce(f32[16,256]{1,0:T(8,128)S(1)} %select_reduce_fusion), channel_id=1, replica_groups=mesh['row'=16,'col'=8] {'row'}, use_global_device_ids=true, to_apply=%region_29.30 | all-reduce | flops 4096 | bytes 32768 | tf_op jit(solution)/shard_map/psum | solution.py:55
  739.4 0.6 copy.19
  740.0 0.6 copy.18
  (19 shorter events, 0.4 us)
Async XLA Ops:
  7.2 76.1 %all-gather.2.cloned.1.call-start = ((), (), s32[]{:S(2)}) async-start(), calls=%async_computation | async-start | bytes 8912896 | tf_op jit(solution)/shard_map/all_gather | solution.py:34
Sparse Core Ops, SparseCore 0:
  10.1 73.0 all-gather.1
where the time goes:
time: 748 us; the launch traced here: 747 us
  blocking collectives  564 us (75%)
  waiting for transfers between devices  71.4 us (10%)
  other arithmetic  54.5 us (7%)
  local copies, waits for them, and re-layouts  30 us (4%)
  between operations  14.3 us (2%)
  matrix products  13.5 us (2%)
    pmax x3, blocking collectives, on_device(): col_high = lax.pmax(local_top, 'row')  211 us
    psum x3, blocking collectives, on_device(): col_total = lax.psum(col_sum, 'row')  209 us
    pmax x3, blocking collectives, on_device(): highest = lax.pmax(row_top, 'col')  73.1 us
    all_gather x1, waiting for transfers between devices, on_device(): lax.all_gather(target_points, 'row', axis=1, tiled=True)  70.8 us
    psum x3, blocking collectives, on_device(): total = lax.psum(local_sum, 'col')  70.7 us
    reduce_sum x3, other arithmetic, on_device(): sums = jnp.sum(jnp.exp(columns - slot_ref[:, :, None, :]), axis=2)  15.4 us
  transfers between devices with their start and end apart: 1, of which 1 were waited for; matrix products, arithmetic and copies ran while one was open for 1% of the time, Pallas kernels for 0%

commit v1 on v0

--- a/solution.py
+++ b/solution.py
@@ -7,6 +7,27 @@
 TILE = 256
 ITERS = 3
 masked_score = -1e30
+
+
+def collect(shard, axis, dim):
+    peers, index, rows = (lax.axis_size(axis), lax.axis_index(axis), shard.shape[dim])
+    right = [(i, (i + 1) % peers) for i in range(peers)]
+    left = [(i, (i - 1) % peers) for i in range(peers)]
+    out = jnp.zeros((*shard.shape[:dim], peers * rows, *shard.shape[dim + 1 :]), shard.dtype)
+    out = lax.dynamic_update_slice_in_dim(out, shard, index * rows, axis=dim)
+    from_left = from_right = shard
+    half = peers // 2
+    for step in range(1, half + 1):
+        from_left = lax.ppermute(from_left, axis, right)
+        out = lax.dynamic_update_slice_in_dim(
+            out, from_left, (index - step) % peers * rows, axis=dim
+        )
+        if step < peers - half:
+            from_right = lax.ppermute(from_right, axis, left)
+            out = lax.dynamic_update_slice_in_dim(
+                out, from_right, (index + step) % peers * rows, axis=dim
+            )
+    return out
 
 
 def cost_terms(piece, source_points, tile_index):
@@ -29,12 +50,7 @@
     target_pot = jnp.zeros((col_tiles, TILE), jnp.float32)
     source_pot = jnp.zeros((tiles_per_row, TILE), jnp.float32)
     for iteration in range(ITERS):
-        cost = (
-            cost_terms(
-                lax.all_gather(target_points, "row", axis=1, tiled=True), source_points, tile_index
-            )
-            * scale
-        )
+        cost = cost_terms(collect(target_points, "row", 1), source_points, tile_index) * scale
         scores = cost + target_pot[tile_index][:, :, None, :]
         scores = jnp.where(live[:, :, None, None], scores, masked_score)
         row_top = jnp.max(scores, axis=(1, 3))

time: 748 us -> 960 us (1.28); the launches traced: 747 us -> 950 us
  local copies, waits for them, and re-layouts: 30 us -> 216 us
  starting transfers between devices: 0.04 us -> 37.5 us
  between operations: 14.3 us -> 1.65 us
    dynamic_update_slice x0 -> x16, local copies, waits for them, and re-layouts: none -> 175 us  [the longest x8 86.8 us: collect(): lax.dynamic_update_slice_in_dim(out, from_left, (index - step) % peers *...]
    all_gather x1 -> x0, waiting for transfers between devices: 70.8 us -> none  [on_device(): lax.all_gather(target_points, 'row', axis=1, tiled=True)]
    ppermute x0 -> x15, waiting for transfers between devices: none -> 62.5 us  [the longest x8 62.5 us: collect(): from_left = lax.ppermute(from_left, axis, right)]
    ppermute x0 -> x15, starting transfers between devices: none -> 37.5 us  [the longest x7 35.8 us: collect(): from_right = lax.ppermute(from_right, axis, left)]
    ppermute x0 -> x15, local copies, waits for them, and re-layouts: none -> 16.6 us  [the longest x8 9 us: collect(): from_left = lax.ppermute(from_left, axis, right)]
    all_gather x1 -> x0, local copies, waits for them, and re-layouts: 12 us -> none  [on_device(): lax.all_gather(target_points, 'row', axis=1, tiled=True)]
  transfers between devices with their start and end apart: 1 -> 15, of which waited for: 1 -> 7; matrix products, arithmetic and copies ran while one was open for 1% -> 20% of each run, Pallas kernels for 0% -> 0%
where the time goes in v1:
time: 960 us; the launch traced here: 950 us
  blocking collectives  565 us (59%)
  local copies, waits for them, and re-layouts  216 us (22%)
  waiting for transfers between devices  62.5 us (7%)
  other arithmetic  53.8 us (6%)
  starting transfers between devices  37.5 us (4%)
  matrix products  13.5 us (1%)
    pmax x3, blocking collectives, on_device(): col_high = lax.pmax(local_top, 'row')  214 us
    psum x3, blocking collectives, on_device(): col_total = lax.psum(col_sum, 'row')  209 us
    dynamic_update_slice x8, local copies, waits for them, and re-layouts, collect(): lax.dynamic_update_slice_in_dim(out, from_left, (index - step) % peers *...  86.8 us
    dynamic_update_slice x7, local copies, waits for them, and re-layouts, collect(): lax.dynamic_update_slice_in_dim(out, from_right, (index + step) % peers *...  77.9 us
    pmax x3, blocking collectives, on_device(): highest = lax.pmax(row_top, 'col')  71.4 us
    psum x3, blocking collectives, on_device(): total = lax.psum(local_sum, 'col')  70.9 us
    ppermute x8, waiting for transfers between devices, collect(): from_left = lax.ppermute(from_left, axis, right)  62.5 us
    ppermute x7, starting transfers between devices, collect(): from_right = lax.ppermute(from_right, axis, left)  35.8 us
  transfers between devices with their start and end apart: 15, of which 7 were waited for; matrix products, arithmetic and copies ran while one was open for 20% of the time, Pallas kernels for 0%

profile of v1, /device:TPU:0, one launch (start us, length us, event | category | flops | bytes accessed | tf_op | source)
XLA Modules:
  0.0 949.5 jit_solution(14964658838885799941)
XLA Ops:
  6.1 12.1 %collective-permute-done = bf16[4096,64]{0,1:T(8,128)(2,1)S(1)} collective-permute-done((bf16[4096,64]{0,1:T(8,128)(2,1)}, bf16[4096,64]{0,1:T(8,128)(2,1)S(1)}, u32[]{:S(2)}, u32[]{:S(2)}) %collective-permute-start) | collective-permute-done | bytes 524320 | tf_op jit(solution)/shard_map/ppermute | solution.py:21
  18.1 5.3 collective-permute-start.3
  23.5 11.0 %collective-permute-done.2 = bf16[4096,64]{0,1:T(8,128)(2,1)S(1)} collective-permute-done((bf16[4096,64]{0,1:T(8,128)(2,1)S(1)}, bf16[4096,64]{0,1:T(8,128)(2,1)S(1)}, u32[]{:S(2)}, u32[]{:S(2)}) %collective-permute-start.2) | collective-permute-done | bytes 524320 | tf_op jit(solution)/shard_map/ppermute | solution.py:21
  34.5 5.3 collective-permute-start.5
  39.9 10.1 %collective-permute-done.4 = bf16[4096,64]{0,1:T(8,128)(2,1)S(1)} collective-permute-done((bf16[4096,64]{0,1:T(8,128)(2,1)S(1)}, bf16[4096,64]{0,1:T(8,128)(2,1)S(1)}, u32[]{:S(2)}, u32[]{:S(2)}) %collective-permute-start.4) | collective-permute-done | bytes 524320 | tf_op jit(solution)/shard_map/ppermute | solution.py:21
  50.0 5.3 collective-permute-start.7
  55.3 9.2 collective-permute-done.6
  64.5 5.3 collective-permute-start.9
  69.9 8.3 collective-permute-done.8
  78.1 5.3 collective-permute-start.11
  83.5 7.4 collective-permute-done.10
  94.3 5.4 collective-permute-start.13
  110.7 10.7 %dynamic_update_slice.32 = bf16[4096,1024]{1,0:T(8,128)(2,1)} dynamic-update-slice(bf16[4096,1024]{1,0:T(8,128)(2,1)} %broadcast.104, bf16[4096,64]{1,0:T(8,128)(2,1)S(1)} %copy.28, s32[]{:T(128)} %constant.158.clone.1, s32[]{:T(128)S(6)} %select_n.270) | dynamic-update-slice | bytes 1048580 | tf_op jit(solution)/shard_map/dynamic_update_slice | solution.py:17
  123.1 11.0 %dynamic_update_slice.33 = bf16[4096,1024]{1,0:T(8,128)(2,1)} dynamic-update-slice(bf16[4096,1024]{1,0:T(8,128)(2,1)} %dynamic_update_slice.32, bf16[4096,64]{1,0:T(8,128)(2,1)S(1)} %copy.29, s32[]{:T(128)} %constant.158.clone.1, s32[]{:T(128)S(6)} %select_n.272) | dynamic-update-slice | bytes 1048580 | tf_op jit(solution)/shard_map/dynamic_update_slice | solution.py:22
  134.6 11.8 %dynamic_update_slice.34 = bf16[4096,1024]{1,0:T(8,128)(2,1)} dynamic-update-slice(bf16[4096,1024]{1,0:T(8,128)(2,1)} %dynamic_update_slice.33, bf16[4096,64]{1,0:T(8,128)(2,1)S(1)} %copy.30, s32[]{:T(128)} %constant.158.clone.1, s32[]{:T(128)S(6)} %select_n.274) | dynamic-update-slice | bytes 1048580 | tf_op jit(solution)/shard_map/dynamic_update_slice | solution.py:27
  146.9 9.4 dynamic_update_slice.35
  157.9 10.2 %dynamic_update_slice.36 = bf16[4096,1024]{1,0:T(8,128)(2,1)} dynamic-update-slice(bf16[4096,1024]{1,0:T(8,128)(2,1)} %dynamic_update_slice.35, bf16[4096,64]{1,0:T(8,128)(2,1)S(1)} %copy.32, s32[]{:T(128)} %constant.158.clone.1, s32[]{:T(128)S(6)} %select_n.278) | dynamic-update-slice | bytes 1048580 | tf_op jit(solution)/shard_map/dynamic_update_slice | solution.py:27
  169.7 11.8 %dynamic_update_slice.37 = bf16[4096,1024]{1,0:T(8,128)(2,1)} dynamic-update-slice(bf16[4096,1024]{1,0:T(8,128)(2,1)} %dynamic_update_slice.36, bf16[4096,64]{1,0:T(8,128)(2,1)S(1)} %copy.33, s32[]{:T(128)} %constant.158.clone.1, s32[]{:T(128)S(6)} %select_n.280) | dynamic-update-slice | bytes 1048580 | tf_op jit(solution)/shard_map/dynamic_update_slice | solution.py:22
  183.0 11.8 %dynamic_update_slice.38 = bf16[4096,1024]{1,0:T(8,128)(2,1)} dynamic-update-slice(bf16[4096,1024]{1,0:T(8,128)(2,1)} %dynamic_update_slice.37, bf16[4096,64]{1,0:T(8,128)(2,1)S(1)} %copy.34, s32[]{:T(128)} %constant.158.clone.1, s32[]{:T(128)S(6)} %select_n.282) | dynamic-update-slice | bytes 1048580 | tf_op jit(solution)/shard_map/dynamic_update_slice | solution.py:27
  195.2 10.3 %dynamic_update_slice.39 = bf16[4096,1024]{1,0:T(8,128)(2,1)} dynamic-update-slice(bf16[4096,1024]{1,0:T(8,128)(2,1)} %dynamic_update_slice.38, bf16[4096,64]{1,0:T(8,128)(2,1)S(1)} %copy.35, s32[]{:T(128)} %constant.158.clone.1, s32[]{:T(128)S(6)} %select_n.284) | dynamic-update-slice | bytes 1048580 | tf_op jit(solution)/shard_map/dynamic_update_slice | solution.py:22
  206.1 10.3 %dynamic_update_slice.40 = bf16[4096,1024]{1,0:T(8,128)(2,1)} dynamic-update-slice(bf16[4096,1024]{1,0:T(8,128)(2,1)} %dynamic_update_slice.39, bf16[4096,64]{1,0:T(8,128)(2,1)S(1)} %copy.36, s32[]{:T(128)} %constant.158.clone.1, s32[]{:T(128)S(6)} %select_n.286) | dynamic-update-slice | bytes 1048580 | tf_op jit(solution)/shard_map/dynamic_update_slice | solution.py:27
  217.8 11.8 %dynamic_update_slice.41 = bf16[4096,1024]{1,0:T(8,128)(2,1)} dynamic-update-slice(bf16[4096,1024]{1,0:T(8,128)(2,1)} %dynamic_update_slice.40, bf16[4096,64]{1,0:T(8,128)(2,1)S(1)} %copy.37, s32[]{:T(128)} %constant.158.clone.1, s32[]{:T(128)S(6)} %select_n.288) | dynamic-update-slice | bytes 1048580 | tf_op jit(solution)/shard_map/dynamic_update_slice | solution.py:22
  231.1 11.8 %dynamic_update_slice.42 = bf16[4096,1024]{1,0:T(8,128)(2,1)} dynamic-update-slice(bf16[4096,1024]{1,0:T(8,128)(2,1)} %dynamic_update_slice.41, bf16[4096,64]{1,0:T(8,128)(2,1)S(1)} %copy.38, s32[]{:T(128)} %constant.158.clone.1, s32[]{:T(128)S(6)} %select_n.290) | dynamic-update-slice | bytes 1048580 | tf_op jit(solution)/shard_map/dynamic_update_slice | solution.py:27
  244.4 10.3 %dynamic_update_slice.43 = bf16[4096,1024]{1,0:T(8,128)(2,1)} dynamic-update-slice(bf16[4096,1024]{1,0:T(8,128)(2,1)} %dynamic_update_slice.42, bf16[4096,64]{1,0:T(8,128)(2,1)S(1)} %copy.39, s32[]{:T(128)} %constant.158.clone.1, s32[]{:T(128)S(6)} %select_n.292) | dynamic-update-slice | bytes 1048580 | tf_op jit(solution)/shard_map/dynamic_update_slice | solution.py:22
  255.2 10.3 %dynamic_update_slice.44 = bf16[4096,1024]{1,0:T(8,128)(2,1)} dynamic-update-slice(bf16[4096,1024]{1,0:T(8,128)(2,1)} %dynamic_update_slice.43, bf16[4096,64]{1,0:T(8,128)(2,1)S(1)} %copy.40, s32[]{:T(128)} %constant.158.clone.1, s32[]{:T(128)S(6)} %select_n.294) | dynamic-update-slice | bytes 1048580 | tf_op jit(solution)/shard_map/dynamic_update_slice | solution.py:27
  266.0 11.8 %dynamic_update_slice.45 = bf16[4096,1024]{1,0:T(8,128)(2,1)} dynamic-update-slice(bf16[4096,1024]{1,0:T(8,128)(2,1)} %dynamic_update_slice.44, bf16[4096,64]{1,0:T(8,128)(2,1)S(1)} %copy.41, s32[]{:T(128)} %constant.158.clone.1, s32[]{:T(128)S(6)} %select_n.296) | dynamic-update-slice | bytes 1048580 | tf_op jit(solution)/shard_map/dynamic_update_slice | solution.py:22
  279.3 11.7 %dynamic_update_slice.46 = bf16[4096,1024]{1,0:T(8,128)(2,1)} dynamic-update-slice(bf16[4096,1024]{1,0:T(8,128)(2,1)} %dynamic_update_slice.45, bf16[4096,64]{1,0:T(8,128)(2,1)S(1)} %copy.42, s32[]{:T(128)} %constant.158.clone.1, s32[]{:T(128)S(6)} %select_n.298) | dynamic-update-slice | bytes 1048580 | tf_op jit(solution)/shard_map/dynamic_update_slice | solution.py:27
  292.6 10.4 %dynamic_update_slice.47 = bf16[4096,1024]{1,0:T(8,128)(2,1)} dynamic-update-slice(bf16[4096,1024]{1,0:T(8,128)(2,1)} %dynamic_update_slice.46, bf16[4096,64]{1,0:T(8,128)(2,1)S(1)} %copy.43, s32[]{:T(128)} %constant.158.clone.1, s32[]{:T(128)S(6)} %select_n.300) | dynamic-update-slice | bytes 1048580 | tf_op jit(solution)/shard_map/dynamic_update_slice | solution.py:22
  303.0 10.6 %gather_fusion = bf16[32,256,1024]{2,1,0:T(8,128)(2,1)} fusion(bf16[16,256,1024]{2,1,0:T(8,128)(2,1)} %bitcast.57, s32[1024]{0:T(1024)S(1)} %pad_clamp_fusion), kind=kCustom, calls=%fused_computation | custom fusion | bytes 33554560 | tf_op jit(solution)/shard_map/gather | solution.py:37
  313.7 13.5 %bitcast_reduce_fusion.5 = (f32[16,256]{1,0:T(8,128)S(1)}, f32[16,2,256,256]{3,2,1,0:T(8,128)}) fusion(f32[16,2,256]{2,1,0:T(2,128)S(1)} %reshape.108, pred[16,2]{1,0:T(8,128)(4,1)S(1)} %iota_compare_fusion, bf16[16,2,256,1024]{3,2,1,0:T(8,128)(2,1)} %bitcast.58, bf16[16,256,1024,1]{2,1,3,0:T(8,128)(2,1)} %bitcast.63), kind=kOutput, calls=%fused_computation.28 | convolution fusion | flops 4303351808 | bytes 33603616 | tf_op jit(solution)/shard_map/rad,rkbd->rkab/dot_general | solution.py:38
  327.1 24.3 %pmax.42 = f32[16,256]{1,0:T(8,128)S(1)} all-reduce(f32[16,256]{1,0:T(8,128)S(1)} %get-tuple-element.2), channel_id=1, replica_groups=mesh['row'=16,'col'=8] {'col'}, use_global_device_ids=true, to_apply=%region_1.2 | all-reduce | flops 4096 | bytes 32768 | tf_op jit(solution)/shard_map/pmax | solution.py:57
  356.1 23.6 %psum.42 = f32[16,256]{1,0:T(8,128)S(1)} all-reduce(f32[16,256]{1,0:T(8,128)S(1)} %fusion.11), channel_id=1, replica_groups=mesh['row'=16,'col'=8] {'col'}, use_global_device_ids=true, to_apply=%region_3.4 | all-reduce | flops 4096 | bytes 32768 | tf_op jit(solution)/shard_map/psum | solution.py:59
  379.6 4.7 bitcast_reduce_fusion.4
  384.4 74.7 %pmax.43 = f32[16,256]{1,0:T(8,128)S(1)} all-reduce(f32[16,256]{1,0:T(8,128)S(1)} %select_reduce_fusion.5), channel_id=1, replica_groups=mesh['row'=16,'col'=8] {'row'}, use_global_device_ids=true, to_apply=%region_6.7 | all-reduce | flops 4096 | bytes 32768 | tf_op jit(solution)/shard_map/pmax | solution.py:67
  459.8 5.1 fusion.9
  465.1 69.5 %psum.43 = f32[16,256]{1,0:T(8,128)S(1)} all-reduce(f32[16,256]{1,0:T(8,128)S(1)} %select_reduce_fusion.4), channel_id=1, replica_groups=mesh['row'=16,'col'=8] {'row'}, use_global_device_ids=true, to_apply=%region_9.10 | all-reduce | flops 4096 | bytes 32768 | tf_op jit(solution)/shard_map/psum | solution.py:71
  539.7 23.6 %pmax.44 = f32[16,256]{1,0:T(8,128)S(1)} all-reduce(f32[16,256]{1,0:T(8,128)S(1)} %bitcast_reduce_fusion.3), channel_id=1, replica_groups=mesh['row'=16,'col'=8] {'col'}, use_global_device_ids=true, to_apply=%region_11.12 | all-reduce | flops 4096 | bytes 32768 | tf_op jit(solution)/shard_map/pmax | solution.py:57
  567.9 23.8 %psum.44 = f32[16,256]{1,0:T(8,128)S(1)} all-reduce(f32[16,256]{1,0:T(8,128)S(1)} %fusion.7), channel_id=1, replica_groups=mesh['row'=16,'col'=8] {'col'}, use_global_device_ids=true, to_apply=%region_13.14 | all-reduce | flops 4096 | bytes 32768 | tf_op jit(solution)/shard_map/psum | solution.py:59
  591.7 4.7 bitcast_reduce_fusion.2
  596.5 69.5 %pmax.45 = f32[16,256]{1,0:T(8,128)S(1)} all-reduce(f32[16,256]{1,0:T(8,128)S(1)} %select_reduce_fusion.3), channel_id=1, replica_groups=mesh['row'=16,'col'=8] {'row'}, use_global_device_ids=true, to_apply=%region_16.17 | all-reduce | flops 4096 | bytes 32768 | tf_op jit(solution)/shard_map/pmax | solution.py:67
  666.6 5.1 fusion.5
  671.9 69.5 %psum.45 = f32[16,256]{1,0:T(8,128)S(1)} all-reduce(f32[16,256]{1,0:T(8,128)S(1)} %select_reduce_fusion.2), channel_id=1, replica_groups=mesh['row'=16,'col'=8] {'row'}, use_global_device_ids=true, to_apply=%region_19.20 | all-reduce | flops 4096 | bytes 32768 | tf_op jit(solution)/shard_map/psum | solution.py:71
  746.5 23.6 %pmax.46 = f32[16,256]{1,0:T(8,128)S(1)} all-reduce(f32[16,256]{1,0:T(8,128)S(1)} %bitcast_reduce_fusion.1), channel_id=1, replica_groups=mesh['row'=16,'col'=8] {'col'}, use_global_device_ids=true, to_apply=%region_21.22 | all-reduce | flops 4096 | bytes 32768 | tf_op jit(solution)/shard_map/pmax | solution.py:57
  774.7 23.6 %psum.46 = f32[16,256]{1,0:T(8,128)S(1)} all-reduce(f32[16,256]{1,0:T(8,128)S(1)} %fusion.3), channel_id=1, replica_groups=mesh['row'=16,'col'=8] {'col'}, use_global_device_ids=true, to_apply=%region_23.24 | all-reduce | flops 4096 | bytes 32768 | tf_op jit(solution)/shard_map/psum | solution.py:59
  798.3 4.7 bitcast_reduce_fusion
  803.1 69.5 %pmax.47 = f32[16,256]{1,0:T(8,128)S(1)} all-reduce(f32[16,256]{1,0:T(8,128)S(1)} %select_reduce_fusion.1), channel_id=1, replica_groups=mesh['row'=16,'col'=8] {'row'}, use_global_device_ids=true, to_apply=%region_26.27 | all-reduce | flops 4096 | bytes 32768 | tf_op jit(solution)/shard_map/pmax | solution.py:67
  873.3 5.1 fusion.1
  878.5 69.5 %psum.47 = f32[16,256]{1,0:T(8,128)S(1)} all-reduce(f32[16,256]{1,0:T(8,128)S(1)} %select_reduce_fusion), channel_id=1, replica_groups=mesh['row'=16,'col'=8] {'row'}, use_global_device_ids=true, to_apply=%region_29.30 | all-reduce | flops 4096 | bytes 32768 | tf_op jit(solution)/shard_map/psum | solution.py:71
  (98 shorter events, 64.2 us)
Async XLA Ops:
  0.6 120.8 %copy-start.9 = (s32[16,1]{0,1:T(1,128)S(1)}, s32[16,1]{0,1:T(1,128)}, u32[]{:S(2)}) copy-start(s32[16,1]{0,1:T(1,128)} %param.11) | copy-start | bytes 196
  0.6 17.5 %collective-permute-start = (bf16[4096,64]{0,1:T(8,128)(2,1)}, bf16[4096,64]{0,1:T(8,128)(2,1)S(1)}, u32[]{:S(2)}, u32[]{:S(2)}) collective-permute-start(bf16[4096,64]{0,1:T(8,128)(2,1)} %param.7), channel_id=1, source_target_pairs={{0,8},{8,16},{16,24},{24,32},{32,40},{40,48},{48,56},{56,64},{64,7... | collective-permute-start | bytes 1572872 | tf_op jit(solution)/shard_map/ppermute | solution.py:21
  2.4 15.8 %collective-permute-start.1 = (bf16[4096,64]{0,1:T(8,128)(2,1)}, bf16[4096,64]{0,1:T(8,128)(2,1)S(1)}, u32[]{:S(2)}, u32[]{:S(2)}) collective-permute-start(bf16[4096,64]{0,1:T(8,128)(2,1)} %param.7), channel_id=1, source_target_pairs={{0,120},{8,0},{16,8},{24,16},{32,24},{40,32},{48,40},{56,48},{64,5... | collective-permute-start | bytes 1572872 | tf_op jit(solution)/shard_map/ppermute | solution.py:26
  18.1 65.3 %copy-start = (bf16[4096,64]{0,1:T(8,128)(2,1)}, bf16[4096,64]{0,1:T(8,128)(2,1)S(1)}, u32[]{:S(2)}) copy-start(bf16[4096,64]{0,1:T(8,128)(2,1)S(1)} %collective-permute-done) | copy-start | bytes 1572868
  18.1 16.4 %collective-permute-start.2 = (bf16[4096,64]{0,1:T(8,128)(2,1)S(1)}, bf16[4096,64]{0,1:T(8,128)(2,1)S(1)}, u32[]{:S(2)}, u32[]{:S(2)}) collective-permute-start(bf16[4096,64]{0,1:T(8,128)(2,1)S(1)} %collective-permute-done), channel_id=1, source_target_pairs={{0,8},{8,16},{16,24},{24,32},{32,40},{40,48},{48,56},{56,64},{64,7... | collective-permute-start | bytes 1572872 | tf_op jit(solution)/shard_map/ppermute | solution.py:21
  18.1 16.4 %collective-permute-start.3 = (bf16[4096,64]{0,1:T(8,128)(2,1)S(1)}, bf16[4096,64]{0,1:T(8,128)(2,1)S(1)}, u32[]{:S(2)}, u32[]{:S(2)}) collective-permute-start(bf16[4096,64]{0,1:T(8,128)(2,1)S(1)} %collective-permute-done.1), channel_id=1, source_target_pairs={{0,120},{8,0},{16,8},{24,16},{32,24},{40,32},{48,40},{56,48},{64,5... | collective-permute-start | bytes 1572872 | tf_op jit(solution)/shard_map/ppermute | solution.py:26
  34.5 15.5 %collective-permute-start.4 = (bf16[4096,64]{0,1:T(8,128)(2,1)S(1)}, bf16[4096,64]{0,1:T(8,128)(2,1)S(1)}, u32[]{:S(2)}, u32[]{:S(2)}) collective-permute-start(bf16[4096,64]{0,1:T(8,128)(2,1)S(1)} %collective-permute-done.2), channel_id=1, source_target_pairs={{0,8},{8,16},{16,24},{24,32},{32,40},{40,48},{48,56},{56,64},{64,7... | collective-permute-start | bytes 1572872 | tf_op jit(solution)/shard_map/ppermute | solution.py:21
  34.5 43.6 %copy-start.1 = (bf16[4096,64]{0,1:T(8,128)(2,1)}, bf16[4096,64]{0,1:T(8,128)(2,1)S(1)}, u32[]{:S(2)}) copy-start(bf16[4096,64]{0,1:T(8,128)(2,1)S(1)} %collective-permute-done.3) | copy-start | bytes 1572868
  34.5 15.5 %collective-permute-start.5 = (bf16[4096,64]{0,1:T(8,128)(2,1)S(1)}, bf16[4096,64]{0,1:T(8,128)(2,1)S(1)}, u32[]{:S(2)}, u32[]{:S(2)}) collective-permute-start(bf16[4096,64]{0,1:T(8,128)(2,1)S(1)} %collective-permute-done.3), channel_id=1, source_target_pairs={{0,120},{8,0},{16,8},{24,16},{32,24},{40,32},{48,40},{56,48},{64,5... | collective-permute-start | bytes 1572872 | tf_op jit(solution)/shard_map/ppermute | solution.py:26
  50.0 41.0 %copy-start.2 = (bf16[4096,64]{0,1:T(8,128)(2,1)}, bf16[4096,64]{0,1:T(8,128)(2,1)S(1)}, u32[]{:S(2)}) copy-start(bf16[4096,64]{0,1:T(8,128)(2,1)S(1)} %collective-permute-done.4) | copy-start | bytes 1572868
  50.0 14.5 %collective-permute-start.6 = (bf16[4096,64]{0,1:T(8,128)(2,1)S(1)}, bf16[4096,64]{0,1:T(8,128)(2,1)S(1)}, u32[]{:S(2)}, u32[]{:S(2)}) collective-permute-start(bf16[4096,64]{0,1:T(8,128)(2,1)S(1)} %collective-permute-done.4), channel_id=1, source_target_pairs={{0,8},{8,16},{16,24},{24,32},{32,40},{40,48},{48,56},{56,64},{64,7... | collective-permute-start | bytes 1572872 | tf_op jit(solution)/shard_map/ppermute | solution.py:21
  50.0 41.0 %copy-start.3 = (bf16[4096,64]{0,1:T(8,128)(2,1)}, bf16[4096,64]{0,1:T(8,128)(2,1)S(1)}, u32[]{:S(2)}) copy-start(bf16[4096,64]{0,1:T(8,128)(2,1)S(1)} %collective-permute-done.5) | copy-start | bytes 1572868
  50.0 14.5 %collective-permute-start.7 = (bf16[4096,64]{0,1:T(8,128)(2,1)S(1)}, bf16[4096,64]{0,1:T(8,128)(2,1)S(1)}, u32[]{:S(2)}, u32[]{:S(2)}) collective-permute-start(bf16[4096,64]{0,1:T(8,128)(2,1)S(1)} %collective-permute-done.5), channel_id=1, source_target_pairs={{0,120},{8,0},{16,8},{24,16},{32,24},{40,32},{48,40},{56,48},{64,5... | collective-permute-start | bytes 1572872 | tf_op jit(solution)/shard_map/ppermute | solution.py:26
  64.5 26.4 %copy-start.4 = (bf16[4096,64]{0,1:T(8,128)(2,1)}, bf16[4096,64]{0,1:T(8,128)(2,1)S(1)}, u32[]{:S(2)}) copy-start(bf16[4096,64]{0,1:T(8,128)(2,1)S(1)} %collective-permute-done.6) | copy-start | bytes 1572868
  64.5 13.6 %collective-permute-start.8 = (bf16[4096,64]{0,1:T(8,128)(2,1)S(1)}, bf16[4096,64]{0,1:T(8,128)(2,1)S(1)}, u32[]{:S(2)}, u32[]{:S(2)}) collective-permute-start(bf16[4096,64]{0,1:T(8,128)(2,1)S(1)} %collective-permute-done.6), channel_id=1, source_target_pairs={{0,8},{8,16},{16,24},{24,32},{32,40},{40,48},{48,56},{56,64},{64,7... | collective-permute-start | bytes 1572872 | tf_op jit(solution)/shard_map/ppermute | solution.py:21
  64.5 26.4 %copy-start.6 = (bf16[4096,64]{0,1:T(8,128)(2,1)}, bf16[4096,64]{0,1:T(8,128)(2,1)S(1)}, u32[]{:S(2)}) copy-start(bf16[4096,64]{0,1:T(8,128)(2,1)S(1)} %collective-permute-done.7) | copy-start | bytes 1572868
  64.5 13.6 %collective-permute-start.9 = (bf16[4096,64]{0,1:T(8,128)(2,1)S(1)}, bf16[4096,64]{0,1:T(8,128)(2,1)}, u32[]{:S(2)}, u32[]{:S(2)}) collective-permute-start(bf16[4096,64]{0,1:T(8,128)(2,1)S(1)} %collective-permute-done.7), channel_id=1, source_target_pairs={{0,120},{8,0},{16,8},{24,16},{32,24},{40,32},{48,40},{56,48},{64,5... | collective-permute-start | bytes 1572872 | tf_op jit(solution)/shard_map/ppermute | solution.py:26
  78.1 12.8 %copy-start.8 = (bf16[4096,64]{0,1:T(8,128)(2,1)}, bf16[4096,64]{0,1:T(8,128)(2,1)S(1)}, u32[]{:S(2)}) copy-start(bf16[4096,64]{0,1:T(8,128)(2,1)S(1)} %collective-permute-done.8) | copy-start | bytes 1572868
  78.1 12.8 %collective-permute-start.10 = (bf16[4096,64]{0,1:T(8,128)(2,1)S(1)}, bf16[4096,64]{0,1:T(8,128)(2,1)}, u32[]{:S(2)}, u32[]{:S(2)}) collective-permute-start(bf16[4096,64]{0,1:T(8,128)(2,1)S(1)} %collective-permute-done.8), channel_id=1, source_target_pairs={{0,8},{8,16},{16,24},{24,32},{32,40},{40,48},{48,56},{56,64},{64,7... | collective-permute-start | bytes 1572872 | tf_op jit(solution)/shard_map/ppermute | solution.py:21
  78.1 16.2 %collective-permute-start.11 = (bf16[4096,64]{0,1:T(8,128)(2,1)}, bf16[4096,64]{0,1:T(8,128)(2,1)S(1)}, u32[]{:S(2)}, u32[]{:S(2)}) collective-permute-start(bf16[4096,64]{0,1:T(8,128)(2,1)} %collective-permute-done.9), channel_id=1, source_target_pairs={{0,120},{8,0},{16,8},{24,16},{32,24},{40,32},{48,40},{56,48},{64,5... | collective-permute-start | bytes 1572872 | tf_op jit(solution)/shard_map/ppermute | solution.py:26
  90.9 13.3 %collective-permute-start.12 = (bf16[4096,64]{0,1:T(8,128)(2,1)}, bf16[4096,64]{0,1:T(8,128)(2,1)S(1)}, u32[]{:S(2)}, u32[]{:S(2)}) collective-permute-start(bf16[4096,64]{0,1:T(8,128)(2,1)} %collective-permute-done.10), channel_id=1, source_target_pairs={{0,8},{8,16},{16,24},{24,32},{32,40},{40,48},{48,56},{56,64},{64,7... | collective-permute-start | bytes 1572872 | tf_op jit(solution)/shard_map/ppermute | solution.py:21
  94.3 183.4 %collective-permute-start.13 = (bf16[4096,64]{0,1:T(8,128)(2,1)S(1)}, bf16[4096,64]{0,1:T(8,128)(2,1)}, u32[]{:S(2)}, u32[]{:S(2)}) collective-permute-start(bf16[4096,64]{0,1:T(8,128)(2,1)S(1)} %collective-permute-done.11), channel_id=1, source_target_pairs={{0,120},{8,0},{16,8},{24,16},{32,24},{40,32},{48,40},{56,48},{64,5... | collective-permute-start | bytes 1572872 | tf_op jit(solution)/shard_map/ppermute | solution.py:26
  104.2 186.9 %collective-permute-start.14 = (bf16[4096,64]{0,1:T(8,128)(2,1)S(1)}, bf16[4096,64]{0,1:T(8,128)(2,1)}, u32[]{:S(2)}, u32[]{:S(2)}) collective-permute-start(bf16[4096,64]{0,1:T(8,128)(2,1)S(1)} %collective-permute-done.12), channel_id=1, source_target_pairs={{0,8},{8,16},{16,24},{24,32},{32,40},{40,48},{48,56},{56,64},{64,7... | collective-permute-start | bytes 1572872 | tf_op jit(solution)/shard_map/ppermute | solution.py:21
  156.3 38.5 %copy-start.5 = (bf16[4096,64]{0,1:T(8,128)(2,1)S(1)}, bf16[4096,64]{0,1:T(8,128)(2,1)}, u32[]{:S(2)}) copy-start(bf16[4096,64]{0,1:T(8,128)(2,1)} %copy-done.4) | copy-start | bytes 1572868
  156.3 49.3 %copy-start.7 = (bf16[4096,64]{0,1:T(8,128)(2,1)S(1)}, bf16[4096,64]{0,1:T(8,128)(2,1)}, u32[]{:S(2)}) copy-start(bf16[4096,64]{0,1:T(8,128)(2,1)} %copy-done.6) | copy-start | bytes 1572868
